TPU v7x, 32 devices: a whole 2x2x4 slice. The times are simulated.
32 devices in a mesh: pole: 2 (over y), col: 4 (over z), row: 4 (over x, core).
Axes of the slice: x: 2, y: 2, z: 4, core: 2. Of those that a mesh axis runs over, the one named last changes fastest.
Arguments:
- ancestor_inverse: bfloat16 [4, 2048, 2048], P('pole', 'col', 'row'), parts along dimension 0, may hold values from -0.125 to 0.125
- panels: bfloat16 [6, 2048, 512], P('pole', 'col'), parts along dimension 0, may hold values from -0.8984375 to 0.8984375
- block_lists: int32 [6, 16], P('pole'), parts along dimension 0, may hold values from -1 to 15, as said below
- diag_inverse: float32 [6, 256, 512], P('pole', ('col', 'row')), parts along dimension 0, may hold values from -6 to 6
Outputs:
- offdiag: bfloat16 [6, 2048, 512], P('pole', ('col', 'row')), parts along dimension 0
- diag_block: float32 [6, 256, 512], P('pole', ('col', 'row')), parts along dimension 0
There are 2 independent parts, one for each index of `pole`. A program takes and returns all parts, laid end to end along the dimension named above; each array names one. Nothing has to cross between parts.
Inputs may be any that keep to these rules, and one draw needn't show every extreme that they name: `block_lists`: in every supernode, the slots of range r hold distinct blocks of r * 4 to r * 4 + 3, filled slots first and -1 after them; every range has at least one filled slot, and some range has all 4 filled.
All inputs are finite; a program needn't handle non-finite values.
Results may differ from a plain program's by a relative error of at most 0.017.
Values may be sent and summed in bfloat16 or wider, within the bound.
A program may use at most 64 MiB of HBM per device.

v0:
```python
import jax
import jax.numpy as jnp
from jax import lax
from jax.sharding import PartitionSpec as P

BS = 128
BPR = 4
CAP = 4


def from_root(value, axis, source):
    kept = jnp.where(lax.axis_index(axis) == source, value, 0).astype(value.dtype)
    return lax.psum(kept, axis)


def complex_product(first, second):
    half = first.shape[1] // 2
    return jnp.concatenate(
        [first[:, :half] - second[:, half:], first[:, half:] + second[:, :half]], axis=1
    )


def on_device(ancestor_inverse, panels, block_lists, diag_inverse):
    here_col = lax.axis_index("col")
    here_row = lax.axis_index("row")
    nsup = panels.shape[0]
    width = panels.shape[2] // 2
    mine = lax.dynamic_slice_in_dim(block_lists, here_col * CAP, CAP, 1)
    theirs = lax.dynamic_slice_in_dim(block_lists, here_row * CAP, CAP, 1)
    row_mask = jnp.repeat((mine >= 0).astype(jnp.bfloat16), BS, axis=1)
    masked = panels * row_mask[:, :, None]
    blocks = ancestor_inverse.reshape(2, BPR, BS, BPR, BS)
    pieces = []
    for k in range(nsup):
        range_rows = from_root(masked[k], "col", here_row)
        row_offset = jnp.clip(mine[k] - here_col * BPR, 0, BPR - 1)
        col_offset = jnp.clip(theirs[k] - here_row * BPR, 0, BPR - 1)
        picked = jnp.take(blocks, row_offset, axis=1)
        picked = jnp.take(picked, col_offset, axis=3).reshape(2, CAP * BS, CAP * BS)
        product_first = jnp.dot(picked[0], range_rows, preferred_element_type=jnp.float32)
        product_second = jnp.dot(picked[1], range_rows, preferred_element_type=jnp.float32)
        pieces.append(
            lax.psum_scatter(
                (
                    complex_product(product_first, product_second)
                    * row_mask[k][:, None].astype(jnp.float32)
                ).astype(jnp.bfloat16),
                "row",
                scatter_dimension=0,
                tiled=True,
            ).astype(jnp.float32)
        )
    summed = jnp.stack(pieces)
    offdiag = (-summed).astype(jnp.bfloat16)
    share = summed.shape[1]
    own_rows = lax.dynamic_slice_in_dim(masked, here_row * share, share, 1)
    dims = (((0,), (0,)), ((), ()))
    updates = []
    for k in range(nsup):
        first = lax.dot_general(
            own_rows[k][:, :width], offdiag[k], dims, preferred_element_type=jnp.float32
        )
        second = lax.dot_general(
            own_rows[k][:, width:], offdiag[k], dims, preferred_element_type=jnp.float32
        )
        updates.append(complex_product(first, second))
    updates = jnp.stack(updates)
    own_update = lax.psum_scatter(updates, ("col", "row"), scatter_dimension=1, tiled=True)
    return (offdiag, diag_inverse - own_update)


def solution(mesh):
    return jax.shard_map(
        on_device,
        mesh=mesh,
        in_specs=(
            P("pole", "col", "row"),
            P("pole", "col", None),
            P("pole", None),
            P("pole", ("col", "row"), None),
        ),
        out_specs=(P("pole", ("col", "row"), None), P("pole", ("col", "row"), None)),
        check_vma=False,
    )
```

profile of v0, /device:TPU:0, one launch (start us, length us, event | category | flops | bytes accessed | tf_op | source)
XLA Modules:
  0.0 228.6 jit_solution(14445422382365033342)
XLA Ops:
  7.2 0.8 compare_convert_fusion
  8.1 1.7 broadcast_multiply_fusion
  9.7 1.2 fusion.23
  11.0 0.6 copy-done.9
  11.8 0.4 copy-done.7
  12.2 1.1 reshape.115
  13.3 1.5 copy.31
  14.8 1.7 gather_fusion.4
  16.5 1.4 select_bitcast_fusion.1
  17.9 1.1 copy.40
  19.0 2.9 %gather_fusion.5 = bf16[4,2,4,128,128]{4,3,2,1,0:T(8,128)(2,1)} fusion(bf16[2,4,128,4,128]{4,2,3,1,0:T(8,128)(2,1)} %copy.40, s32[1024]{0:T(1024)S(1)} %pad_clamp_fusion), kind=kCustom, calls=%fused_computation.5.clone | custom fusion | bytes 2097168 | tf_op jit(solution)/shard_map/jit(_take)/gather | solution.py:39
  21.9 1.4 select_bitcast_fusion
  23.4 1.2 copy.41
  24.6 1.2 copy.42
  25.8 1.7 gather_fusion.2
  27.5 1.6 gather_fusion
  29.1 1.4 select_bitcast_fusion.3
  30.5 1.1 copy.36
  31.6 0.5 copy-done
  32.3 1.0 copy.32
  33.3 2.0 gather_fusion.1
  35.4 0.9 fusion.36
  36.3 0.4 copy.33
  36.8 2.0 gather_fusion.3
  39.0 1.2 copy.37
  40.2 1.2 copy.38
  41.5 0.4 copy.34
  42.0 41.7 %all-reduce.3.cloned.1.call-done = (bf16[512,512]{1,0:T(8,128)(2,1)}, bf16[512,512]{1,0:T(8,128)(2,1)}, bf16[512,512]{1,0:T(8,128)(2,1)}) async-done(((bf16[512,512]{1,0:T(8,128)(2,1)}, bf16[512,512]{1,0:T(8,128)(2,1)}, bf16[512,512]{1,0:T(8,128)(2,1)}), (bf16[512,512]{1,0:T(8,128)(2,1)}, bf16[512,512]{1,0:T(8,128)(2,1)}, bf16[512,512]{1,0:T(8,128)(2,1)})) %all-reduce.3.cloned.1.call-update) | async-done | bytes 1572880 | tf_op jit(solution)/shard_map/psum | solution.py:13
  83.7 1.7 fusion.3
  85.5 0.5 fusion.6
  86.3 1.0 copy.48
  87.4 1.8 fusion.9
  89.2 0.5 fusion.12
  90.1 1.0 copy.46
  91.2 1.6 fusion.15
  92.8 0.5 fusion.18
  93.6 1.0 copy.44
  94.7 13.4 %reduce-scatter.17.cloned.1.call-done = bf16[128,512]{1,0:T(8,128)(2,1)} async-done(((bf16[512,512]{1,0:T(8,128)(2,1)}), bf16[128,512]{1,0:T(8,128)(2,1)}) %reduce-scatter.17.cloned.1.call-update) | async-done | bytes 131088
  108.1 1.0 copy.49
  109.2 23.3 %reduce-scatter.15.cloned.1.call-done = bf16[128,512]{1,0:T(8,128)(2,1)} async-done(((bf16[512,512]{1,0:T(8,128)(2,1)}), bf16[128,512]{1,0:T(8,128)(2,1)}) %reduce-scatter.15.cloned.1.call-update) | async-done | bytes 131088
  132.5 1.0 copy.47
  133.5 23.0 %reduce-scatter.13.cloned.1.call-done = bf16[128,512]{1,0:T(8,128)(2,1)} async-done(((bf16[512,512]{1,0:T(8,128)(2,1)}), bf16[128,512]{1,0:T(8,128)(2,1)}) %reduce-scatter.13.cloned.1.call-update) | async-done | bytes 131088
  156.5 1.0 copy.45
  157.9 0.2 fusion.29
  159.5 1.3 pad_maximum_fusion
  160.9 0.9 copy.43
  161.8 58.7 %reduce-scatter.11.cloned.1.call-done = f32[3,16,512]{2,1,0:T(8,128)} async-done(((f32[3,256,512]{2,1,0:T(8,128)}), f32[3,16,512]{2,1,0:T(8,128)}) %reduce-scatter.11.cloned.1.call-update) | async-done | bytes 98320 | tf_op jit(solution)/shard_map/reduce_scatter | solution.py:68
  220.6 1.5 sub.69
  (64 shorter events, 4.1 us)
Async XLA Ops:
  7.2 76.6 %all-reduce.3.cloned.1.call-start = ((), (), s32[]{:S(2)}) async-start(), calls=%async_computation.8 | async-start | bytes 3145728 | tf_op jit(solution)/shard_map/psum | solution.py:13
  10.9 0.7 copy-start.9
  11.0 1.2 copy-start.7
  11.0 97.2 %reduce-scatter.17.cloned.1.call-start = ((), (), s32[]{:S(2)}) async-start(), calls=%async_computation.7 | async-start | bytes 655360
  30.5 1.6 copy-start
  39.0 2.4 %copy-start.3 = (bf16[1,4,128,4,128]{4,2,1,0,3:T(8,128)(2,1)S(1)}, bf16[1,4,128,4,128]{4,2,1,0,3:T(8,128)(2,1)}, u32[]{:S(2)}) copy-start(bf16[1,4,128,4,128]{4,2,1,0,3:T(8,128)(2,1)} %get-tuple-element.50) | copy-start | bytes 1572868
  41.5 44.0 %copy-start.1 = (bf16[1,4,128,4,128]{4,3,2,1,0:T(4,128)(2,1)S(1)}, bf16[1,4,128,4,128]{4,3,2,1,0:T(4,128)(2,1)}, u32[]{:S(2)}) copy-start(bf16[1,4,128,4,128]{4,3,2,1,0:T(4,128)(2,1)} %copy.41) | copy-start | bytes 1572868
  83.7 1.8 copy-start.6
  87.3 1.8 copy-start.2
  87.4 45.1 %reduce-scatter.15.cloned.1.call-start = ((), (), s32[]{:S(2)}) async-start(), calls=%async_computation.6 | async-start | bytes 655360
  87.4 1.8 copy-start.5
  91.1 1.7 copy-start.4
  91.1 65.4 %reduce-scatter.13.cloned.1.call-start = ((), (), s32[]{:S(2)}) async-start(), calls=%async_computation.5 | async-start | bytes 655360
  94.6 125.9 %reduce-scatter.11.cloned.1.call-start = ((), (), s32[]{:S(2)}) async-start(), calls=%async_computation.4 | async-start | bytes 1671168 | tf_op jit(solution)/shard_map/reduce_scatter | solution.py:68
  160.9 59.7 %copy-start.8 = (f32[3,16,512]{2,1,0:T(8,128)S(1)}, f32[3,16,512]{2,1,0:T(8,128)}, u32[]{:S(2)}) copy-start(f32[3,16,512]{2,1,0:T(8,128)} %param.11) | copy-start | bytes 294916
Sparse Core Ops, SparseCore 0:
  11.1 72.5 all-reduce.2
  87.5 20.5 reduce-scatter.16
  110.8 21.6 reduce-scatter.14
  134.8 21.6 reduce-scatter.12
  161.0 59.4 reduce-scatter.10
where the time goes:
time: 229 us
  waiting for transfers between devices  160 us (70%)
  local copies, waits for them, and re-layouts  33.3 us (15%)
  between operations  14.2 us (6%)
  other arithmetic  12.7 us (6%)
  matrix products  8.01 us (3%)
    unnamed x8, waiting for transfers between devices  59.8 us
    reduce_scatter x1, waiting for transfers between devices, on_device(): lax.psum_scatter(updates, ('col', 'row'), scatter_dimension=1, tiled=True)  58.7 us
    psum x1, waiting for transfers between devices, from_root(): return lax.psum(kept, axis)  41.7 us
    unnamed x29, local copies, waits for them, and re-layouts  8.66 us
    gather x3, local copies, waits for them, and re-layouts, on_device(): picked = jnp.take(picked, col_offset, axis=3).reshape(2, CAP * BS, CAP * BS)  6.84 us
    dot_general x3, matrix products, on_device(): jnp.dot(picked[1], range_rows, preferred_element_type=jnp.float32)  5.09 us
    gather x3, local copies, waits for them, and re-layouts, on_device(): picked = jnp.take(blocks, row_offset, axis=1)  5.01 us
  transfers between devices with their start and end apart: 5, of which 5 were waited for; matrix products, arithmetic and copies ran while one was open for 17% of the time, Pallas kernels for 0%

commit v1 on v0

--- a/solution.py
+++ b/solution.py
@@ -1,11 +1,357 @@
+import functools
+
 import jax
 import jax.numpy as jnp
 from jax import lax
+from jax.experimental import pallas as pl
+from jax.experimental.pallas import tpu as pltpu
 from jax.sharding import PartitionSpec as P
 
 BS = 128
 BPR = 4
 CAP = 4
+CORES = 2
+RELAYED = 2
+MESH = pl.DeviceIdType.MESH
+
+
+def kernel(
+    ncol,
+    lists,
+    inverse,
+    panels,
+    diag_inverse,
+    offdiag,
+    diag_block,
+    listed,
+    relay,
+    turned,
+    term,
+    parts,
+    first_in,
+    second_out,
+    second_in,
+    third_out,
+    third_own,
+    third_in,
+    chain_send,
+    chain_recv,
+    relay_send,
+    relay_recv,
+    cross_send,
+    first_send,
+    first_recv,
+    second_send,
+    second_recv,
+    third_send,
+    third_recv,
+    local_sem,
+):
+    nsup = panels.shape[0]
+    width = panels.shape[3] // 2
+    deep = diag_inverse.shape[1]
+    col = lax.axis_index("col")
+    row = lax.axis_index("row")
+    core = lax.rem(row, CORES)
+    across = row // CORES
+    sibling = across * CORES + (1 - core)
+    opposite = (1 - across) * CORES + core
+    main = range(CAP - RELAYED)
+    relayed = range(CAP - RELAYED, CAP)
+    ways = (1, -1)
+
+    barrier = pltpu.get_barrier_semaphore()
+    for other in (sibling, opposite):
+        pl.semaphore_signal(barrier, inc=1, device_id={"row": other}, device_id_type=MESH)
+    for step in range(1, ncol):
+        pl.semaphore_signal(
+            barrier, inc=1, device_id={"col": lax.rem(col + step, ncol)}, device_id_type=MESH
+        )
+    pl.semaphore_wait(barrier, ncol + 1)
+
+    def along(source, target, send, recv, way):
+        return pltpu.make_async_remote_copy(
+            src_ref=source,
+            dst_ref=target,
+            send_sem=send,
+            recv_sem=recv,
+            device_id={"col": jnp.clip(col + way, 0, ncol - 1)},
+            device_id_type=MESH,
+        )
+
+    def in_row(source, target, send, recv, other):
+        return pltpu.make_async_remote_copy(
+            src_ref=source,
+            dst_ref=target,
+            send_sem=send,
+            recv_sem=recv,
+            device_id={"row": other},
+            device_id_type=MESH,
+        )
+
+    def room(way):
+        return col < ncol - 1 if way > 0 else col > 0
+
+    def beyond(origin, way):
+        return col > origin if way > 0 else col < origin
+
+    def chain_copy(source, k, s, w):
+        return along(
+            source, listed[k].at[s], chain_send.at[k, s, w], chain_recv.at[k, s], ways[w]
+        )
+
+    def relay_copy(source, at, k, s, w):
+        i = s - relayed[0]
+        return along(
+            source.at[k, at], relay.at[k, i], relay_send.at[k, i, w], relay_recv.at[k, i], ways[w]
+        )
+
+    def cross_copy(k, s):
+        i = s - relayed[0]
+        return in_row(relay.at[k, i], listed[k].at[s], cross_send.at[k, i], chain_recv.at[k, s], opposite)
+
+    def own_copy(k):
+        return pltpu.make_async_copy(panels.at[k], listed[k], local_sem.at[k])
+
+    for w, way in enumerate(ways):
+
+        @pl.when((col == row) & room(way))
+        def _():
+            for k in range(nsup):
+                for s in main:
+                    chain_copy(panels.at[k, s], k, s, w).start()
+
+        @pl.when((col == opposite) & room(way))
+        def _():
+            for k in range(nsup):
+                for s in relayed:
+                    relay_copy(panels, s, k, s, w).start()
+
+    @pl.when(col == row)
+    def _():
+        for k in range(nsup):
+            own_copy(k).start()
+
+    for k in range(nsup):
+        rows = jnp.concatenate(
+            [panels[k, x * CORES + c] for c in range(CORES) for x in range(CAP // CORES)], axis=0
+        )
+        turned[k] = rows.T
+
+    @pl.when(col == row)
+    def _():
+        for k in range(nsup):
+            own_copy(k).wait()
+
+    def forward(k):
+        for j in range(CAP):
+            if j < len(main):
+                s = main[j]
+
+                @pl.when(col != row)
+                def _():
+                    chain_copy(listed[k].at[s], k, s, 0).wait_recv()
+
+                for w, way in enumerate(ways):
+
+                    @pl.when(beyond(row, way) & room(way))
+                    def _():
+                        chain_copy(listed[k].at[s], k, s, w).start()
+
+            if j < len(relayed):
+                s = relayed[j]
+
+                @pl.when(col != opposite)
+                def _():
+                    relay_copy(relay, s - relayed[0], k, s, 0).wait_recv()
+                    cross_copy(k, s).start()
+
+                for w, way in enumerate(ways):
+
+                    @pl.when(beyond(opposite, way) & room(way))
+                    def _():
+                        relay_copy(relay, s - relayed[0], k, s, w).start()
+
+        for s in relayed:
+
+            @pl.when(col != row)
+            def _():
+                cross_copy(k, s).wait_recv()
+
+    def first_copy(k):
+        return in_row(
+            parts.at[k, 1 - core], first_in.at[k], first_send.at[k], first_recv.at[k], sibling
+        )
+
+    def second_copy(k):
+        return in_row(
+            second_out.at[k], second_in.at[k], second_send.at[k], second_recv.at[k], opposite
+        )
+
+    def third_copy(k, step):
+        target = lax.rem(col + step, ncol)
+        return pltpu.make_async_remote_copy(
+            src_ref=third_out.at[k, target],
+            dst_ref=third_in.at[k, step - 1],
+            send_sem=third_send.at[k, step - 1],
+            recv_sem=third_recv.at[k, step - 1],
+            device_id={"col": target},
+            device_id_type=MESH,
+        )
+
+    def compute(k):
+        natural = []
+        for b in range(BPR):
+            at = jnp.int32(0)
+            found = jnp.int32(0)
+            for s in range(CAP):
+                hit = lists[k, row * CAP + s] == row * BPR + b
+                at = jnp.where(hit, s, at)
+                found = jnp.where(hit, 1, found)
+            block = listed[k][at]
+            natural.append(block * found.astype(jnp.float32).astype(block.dtype))
+        natural = jnp.concatenate(natural, axis=0)
+        both_planes = inverse[...].reshape(2 * BPR * BS, BPR * BS)
+        product = jnp.dot(both_planes, natural, preferred_element_type=jnp.float32)
+        first, second = product[: BPR * BS], product[BPR * BS :]
+        term[:, :, :width] = (
+            (first[:, :width] - second[:, width:]).astype(term.dtype).reshape(BPR, BS, width)
+        )
+        term[:, :, width:] = (
+            (first[:, width:] + second[:, :width]).astype(term.dtype).reshape(BPR, BS, width)
+        )
+        slots = []
+        for c in range(CORES):
+            for x in range(CAP // CORES):
+                block_id = lists[k, col * CAP + x * CORES + c]
+                filled = (block_id >= 0).astype(jnp.float32).astype(term.dtype)
+                piece = term[jnp.clip(block_id - col * BPR, 0, BPR - 1)] * filled
+                parts[k, c, x, :BS] = piece
+                slots.append(piece)
+        slots = jnp.concatenate(slots, axis=0)
+        update = jnp.dot(turned[k], slots, preferred_element_type=jnp.float32)
+        first, second = update[:width], update[width:]
+        update = jnp.concatenate(
+            [first[:, :width] - second[:, width:], first[:, width:] + second[:, :width]], axis=1
+        ).astype(parts.dtype)
+        for z in range(ncol):
+            for r in range(CAP):
+                at = (z * CAP + r) * deep
+                parts[k, r % CORES, r // CORES, BS + z * deep : BS + (z + 1) * deep] = update[at : at + deep]
+        first_copy(k).start()
+
+    def first_sum(k, x):
+        return parts[k, core, x].astype(jnp.float32) + first_in[k, x].astype(jnp.float32)
+
+    def second_stage(k):
+        first_copy(k).wait_recv()
+        second_out[k] = first_sum(k, 1 - across).astype(second_out.dtype)
+        second_copy(k).start()
+
+    def third_stage(k):
+        second_copy(k).wait_recv()
+        total = first_sum(k, across) + second_in[k].astype(jnp.float32)
+        offdiag[k] = (-total[:BS]).astype(offdiag.dtype)
+        third_own[k] = total[BS:].reshape(ncol, deep, 2 * width)
+        third_out[k] = total[BS:].reshape(ncol, deep, 2 * width).astype(third_out.dtype)
+        for step in range(1, ncol):
+            third_copy(k, step).start()
+
+    def last_stage(k):
+        total = diag_inverse[k] + third_own[k, col]
+        for step in range(1, ncol):
+            third_copy(k, step).wait_recv()
+            total += third_in[k, step - 1].astype(jnp.float32)
+        diag_block[k] = total
+
+    for k in range(nsup):
+        forward(k)
+        if k > 0:
+            second_stage(k - 1)
+        compute(k)
+        if k > 0:
+            third_stage(k - 1)
+    second_stage(nsup - 1)
+    third_stage(nsup - 1)
+    for k in range(nsup):
+        last_stage(k)
+
+    for k in range(nsup):
+        first_copy(k).wait_send()
+        second_copy(k).wait_send()
+        for step in range(1, ncol):
+            third_copy(k, step).wait_send()
+    for w, way in enumerate(ways):
+
+        @pl.when((beyond(row, way) | (col == row)) & room(way))
+        def _():
+            for k in range(nsup):
+                for s in main:
+                    chain_copy(listed[k].at[s], k, s, w).wait_send()
+
+        @pl.when((beyond(opposite, way) | (col == opposite)) & room(way))
+        def _():
+            for k in range(nsup):
+                for s in relayed:
+                    relay_copy(relay, s - relayed[0], k, s, w).wait_send()
+
+    @pl.when(col != opposite)
+    def _():
+        for k in range(nsup):
+            for s in relayed:
+                cross_copy(k, s).wait_send()
+
+
+def fused(ncol, ancestor_inverse, panels, block_lists, diag_inverse):
+    nsup, depth, columns = panels.shape
+    deep = diag_inverse.shape[1]
+    tall = BS + ncol * deep
+    crosses = CAP // CORES
+    narrow, wide = panels.dtype, jnp.float32
+    vmem = pl.BlockSpec(memory_space=pltpu.VMEM)
+    dma = pltpu.SemaphoreType.DMA
+    return pl.pallas_call(
+        functools.partial(kernel, ncol),
+        out_shape=(
+            jax.ShapeDtypeStruct((nsup, BS, columns), narrow),
+            jax.ShapeDtypeStruct(diag_inverse.shape, wide),
+        ),
+        in_specs=[pl.BlockSpec(memory_space=pltpu.SMEM), vmem, vmem, vmem],
+        out_specs=(vmem, vmem),
+        scratch_shapes=[
+            tuple(pltpu.VMEM((CAP, BS, columns), narrow) for _ in range(nsup)),
+            pltpu.VMEM((nsup, RELAYED, BS, columns), narrow),
+            pltpu.VMEM((nsup, columns, depth), narrow),
+            pltpu.VMEM((BPR, BS, columns), narrow),
+            pltpu.VMEM((nsup, CORES, crosses, tall, columns), narrow),
+            pltpu.VMEM((nsup, crosses, tall, columns), narrow),
+            pltpu.VMEM((nsup, tall, columns), narrow),
+            pltpu.VMEM((nsup, tall, columns), narrow),
+            pltpu.VMEM((nsup, ncol, deep, columns), narrow),
+            pltpu.VMEM((nsup, ncol, deep, columns), wide),
+            pltpu.VMEM((nsup, ncol - 1, deep, columns), narrow),
+            dma((nsup, CAP, 2)),
+            dma((nsup, CAP)),
+            dma((nsup, RELAYED, 2)),
+            dma((nsup, RELAYED)),
+            dma((nsup, RELAYED)),
+            dma((nsup,)),
+            dma((nsup,)),
+            dma((nsup,)),
+            dma((nsup,)),
+            dma((nsup, ncol - 1)),
+            dma((nsup, ncol - 1)),
+            dma((nsup,)),
+        ],
+        compiler_params=pltpu.CompilerParams(
+            collective_id=0, has_side_effects=True, vmem_limit_bytes=48 * 1024 * 1024
+        ),
+    )(
+        block_lists,
+        ancestor_inverse,
+        panels.reshape(nsup, CAP, BS, columns),
+        diag_inverse,
+    )
 
 
 def from_root(value, axis, source):
@@ -70,8 +416,16 @@
 
 
 def solution(mesh):
+    ncol, nrow = mesh.shape["col"], mesh.shape["row"]
+
+    def on_mesh(ancestor_inverse, panels, block_lists, diag_inverse):
+        whole_slots = nrow == CAP and ncol == nrow
+        if whole_slots and diag_inverse.shape[1] % 16 == 0:
+            return fused(ncol, ancestor_inverse, panels, block_lists, diag_inverse)
+        return on_device(ancestor_inverse, panels, block_lists, diag_inverse)
+
     return jax.shard_map(
-        on_device,
+        on_mesh,
         mesh=mesh,
         in_specs=(
             P("pole", "col", "row"),

time: 229 us -> 72.1 us (0.31)
  waiting for transfers between devices: 160 us -> 0 us
  Pallas kernels: 0 us -> 65.6 us
  local copies, waits for them, and re-layouts: 33.3 us -> 5.59 us
  between operations: 14.2 us -> 0.65 us
  other arithmetic: 12.7 us -> 0 us
  matrix products: 8.01 us -> 0 us
    pallas_call x0 -> x1, Pallas kernels: none -> 65.6 us  [fused(): pl.pallas_call(functools.partial(kernel, ncol), out_shape=(jax.ShapeDtype...]
    unnamed x8 -> x0, waiting for transfers between devices: 59.8 us -> none
    reduce_scatter x1 -> x0, waiting for transfers between devices: 58.7 us -> none  [on_device(): lax.psum_scatter(updates, ('col', 'row'), scatter_dimension=1, tiled=True)]
    psum x1 -> x0, waiting for transfers between devices: 41.7 us -> none  [from_root(): return lax.psum(kept, axis)]
    gather x6 -> x0, local copies, waits for them, and re-layouts: 11.9 us -> none  [the longest x3 6.84 us: on_device(): picked = jnp.take(picked, col_offset, axis=3).reshape(2, CAP * BS, CAP * BS)]
    dot_general x12 -> x0, matrix products: 8.01 us -> none  [the longest x3 5.09 us: on_device(): jnp.dot(picked[1], range_rows, preferred_element_type=jnp.float32)]
    slice x9 -> x0, local copies, waits for them, and re-layouts: 6.76 us -> none  [the longest x6 3.93 us: on_device(): picked[0]]
    select_n x7 -> x0, other arithmetic: 5.86 us -> none  [the longest x3 2.94 us: on_device(): picked = jnp.take(blocks, row_offset, axis=1)]
  transfers between devices with their start and end apart: 5 -> 0, of which waited for: 5 -> 0; matrix products, arithmetic and copies ran while one was open for 17% -> 0% of each run, Pallas kernels for 0% -> 0%
where the time goes in v1:
time: 72.1 us; the launch traced here: 71.9 us
  Pallas kernels  65.6 us (91%)
  local copies, waits for them, and re-layouts  5.59 us (8%)
    pallas_call x1, Pallas kernels, fused(): pl.pallas_call(functools.partial(kernel, ncol), out_shape=(jax.ShapeDtype...  65.6 us
    unnamed x10, local copies, waits for them, and re-layouts  5.59 us

profile of v1, /device:TPU:0, one launch (start us, length us, event | category | flops | bytes accessed | tf_op | source)
XLA Modules:
  0.0 71.9 jit_solution(18058256054488340702)
XLA Ops:
  0.6 0.0 copy-start
  0.6 1.4 %copy-done = bf16[3,512,512]{2,1,0:T(8,128)(2,1)S(1)} copy-done((bf16[3,512,512]{2,1,0:T(8,128)(2,1)S(1)}, bf16[3,512,512]{2,1,0:T(8,128)(2,1)}, u32[]{:S(2)}) %copy-start) | copy-done | bytes 1572888
  2.0 0.0 copy-start.1
  2.0 1.2 %copy-done.1 = bf16[2,512,512]{2,1,0:T(8,128)(2,1)S(1)} copy-done((bf16[2,512,512]{2,1,0:T(8,128)(2,1)S(1)}, bf16[2,512,512]{2,1,0:T(8,128)(2,1)}, u32[]{:S(2)}) %copy-start.1) | copy-done | bytes 1048600
  3.3 0.0 copy-start.2
  3.3 0.9 %copy-done.2 = f32[3,16,512]{2,1,0:T(8,128)S(1)} copy-done((f32[3,16,512]{2,1,0:T(8,128)S(1)}, f32[3,16,512]{2,1,0:T(8,128)}, u32[]{:S(2)}) %copy-start.2) | copy-done | bytes 98328
  4.2 0.0 copy-start.3
  4.2 0.7 copy-done.3
  4.8 65.6 %shard_map.59 = (bf16[3,128,512]{2,1,0:T(8,128)(2,1)S(1)}, f32[3,16,512]{2,1,0:T(8,128)S(1)}) custom-call(s32[3,16]{1,0:T(4,128)S(1)} %copy-done.3, bf16[2,512,512]{2,1,0:T(8,128)(2,1)S(1)} %copy-done.1, bf16[3,4,128,512]{3,2,1,0:T(8,128)(2,1)S(1)} %bitcast.1, f32[3,16,512]{2,1,0:T(8,128)S(1)} %copy-done.2), custom_call_target="tpu_custom_call" | custom-call | tf_op jit(solution)/shard_map/pallas_call | solution.py:313
  70.5 0.7 %copy.8 = bf16[3,128,512]{2,1,0:T(8,128)(2,1)} copy(bf16[3,128,512]{2,1,0:T(8,128)(2,1)S(1)} %get-tuple-element.4) | data formatting | bytes 786432
  71.2 0.6 copy.9
Async XLA Ops:
  0.6 1.4 %copy-start = (bf16[3,512,512]{2,1,0:T(8,128)(2,1)S(1)}, bf16[3,512,512]{2,1,0:T(8,128)(2,1)}, u32[]{:S(2)}) copy-start(bf16[3,512,512]{2,1,0:T(8,128)(2,1)} %param.5) | copy-start | bytes 4718596
  2.0 1.2 %copy-start.1 = (bf16[2,512,512]{2,1,0:T(8,128)(2,1)S(1)}, bf16[2,512,512]{2,1,0:T(8,128)(2,1)}, u32[]{:S(2)}) copy-start(bf16[2,512,512]{2,1,0:T(8,128)(2,1)} %inverse.1) | copy-start | bytes 3145732
  3.3 0.9 %copy-start.2 = (f32[3,16,512]{2,1,0:T(8,128)S(1)}, f32[3,16,512]{2,1,0:T(8,128)}, u32[]{:S(2)}) copy-start(f32[3,16,512]{2,1,0:T(8,128)} %diag_inverse.1) | copy-start | bytes 294916
  4.2 0.7 copy-start.3

commit v2 on v1

--- a/solution.py
+++ b/solution.py
@@ -11,18 +11,22 @@
 BPR = 4
 CAP = 4
 CORES = 2
-RELAYED = 2
+RELAYED = 1
+TURN = 1
 MESH = pl.DeviceIdType.MESH
 
 
 def kernel(
     ncol,
     lists,
+    inverse_hbm,
+    panels_hbm,
+    diag_hbm,
+    offdiag,
+    diag_block,
     inverse,
     panels,
     diag_inverse,
-    offdiag,
-    diag_block,
     listed,
     relay,
     turned,
@@ -46,9 +50,18 @@
     third_send,
     third_recv,
     local_sem,
+    load_sem,
 ):
     nsup = panels.shape[0]
     width = panels.shape[3] // 2
+    loads = [
+        pltpu.make_async_copy(source, target, load_sem.at[i])
+        for i, (source, target) in enumerate(
+            ((panels_hbm, panels), (inverse_hbm, inverse), (diag_hbm, diag_inverse))
+        )
+    ]
+    for load in loads:
+        load.start()
     deep = diag_inverse.shape[1]
     col = lax.axis_index("col")
     row = lax.axis_index("row")
@@ -95,6 +108,11 @@
     def beyond(origin, way):
         return col > origin if way > 0 else col < origin
 
+    def far(origin, way):
+        return origin < ncol // 2 if way > 0 else origin >= ncol // 2
+
+    carries = (beyond(opposite, 1) & far(opposite, 1)) | (beyond(opposite, -1) & far(opposite, -1))
+
     def chain_copy(source, k, s, w):
         return along(
             source, listed[k].at[s], chain_send.at[k, s, w], chain_recv.at[k, s], ways[w]
@@ -111,27 +129,32 @@
         return in_row(relay.at[k, i], listed[k].at[s], cross_send.at[k, i], chain_recv.at[k, s], opposite)
 
     def own_copy(k):
-        return pltpu.make_async_copy(panels.at[k], listed[k], local_sem.at[k])
-
-    for w, way in enumerate(ways):
-
-        @pl.when((col == row) & room(way))
-        def _():
-            for k in range(nsup):
+        return pltpu.make_async_copy(panels_hbm.at[k], listed[k], local_sem.at[k])
+
+    for k in range(nsup):
+        for w, way in enumerate(ways):
+
+            @pl.when((col == row) & room(way))
+            def _():
                 for s in main:
-                    chain_copy(panels.at[k, s], k, s, w).start()
-
-        @pl.when((col == opposite) & room(way))
-        def _():
-            for k in range(nsup):
+                    chain_copy(panels_hbm.at[k, s], k, s, w).start()
+
+            @pl.when((col == row) & room(way) & jnp.logical_not(far(row, way)))
+            def _():
                 for s in relayed:
-                    relay_copy(panels, s, k, s, w).start()
+                    chain_copy(panels_hbm.at[k, s], k, s, w).start()
+
+            @pl.when((col == opposite) & room(way) & far(opposite, way))
+            def _():
+                for s in relayed:
+                    relay_copy(panels_hbm, s, k, s, w).start()
 
     @pl.when(col == row)
     def _():
         for k in range(nsup):
             own_copy(k).start()
 
+    loads[0].wait()
     for k in range(nsup):
         rows = jnp.concatenate(
             [panels[k, x * CORES + c] for c in range(CORES) for x in range(CAP // CORES)], axis=0
@@ -143,6 +166,9 @@
         for k in range(nsup):
             own_copy(k).wait()
 
+    loads[1].wait()
+    loads[2].wait()
+
     def forward(k):
         for j in range(CAP):
             if j < len(main):
@@ -161,22 +187,31 @@
             if j < len(relayed):
                 s = relayed[j]
 
-                @pl.when(col != opposite)
+                @pl.when(carries)
                 def _():
                     relay_copy(relay, s - relayed[0], k, s, 0).wait_recv()
                     cross_copy(k, s).start()
 
                 for w, way in enumerate(ways):
 
-                    @pl.when(beyond(opposite, way) & room(way))
+                    @pl.when(beyond(opposite, way) & room(way) & far(opposite, way))
                     def _():
                         relay_copy(relay, s - relayed[0], k, s, w).start()
 
+            if k > 0 and j == TURN:
+                second_stage(k - 1)
+
         for s in relayed:
 
             @pl.when(col != row)
             def _():
-                cross_copy(k, s).wait_recv()
+                chain_copy(listed[k].at[s], k, s, 0).wait_recv()
+
+            for w, way in enumerate(ways):
+
+                @pl.when(beyond(row, way) & room(way) & jnp.logical_not(far(row, way)))
+                def _():
+                    chain_copy(listed[k].at[s], k, s, w).start()
 
     def first_copy(k):
         return in_row(
@@ -266,13 +301,10 @@
 
     for k in range(nsup):
         forward(k)
-        if k > 0:
-            second_stage(k - 1)
         compute(k)
-        if k > 0:
-            third_stage(k - 1)
     second_stage(nsup - 1)
-    third_stage(nsup - 1)
+    for k in range(nsup):
+        third_stage(k)
     for k in range(nsup):
         last_stage(k)
 
@@ -289,13 +321,19 @@
                 for s in main:
                     chain_copy(listed[k].at[s], k, s, w).wait_send()
 
-        @pl.when((beyond(opposite, way) | (col == opposite)) & room(way))
+        @pl.when((beyond(row, way) | (col == row)) & room(way) & jnp.logical_not(far(row, way)))
+        def _():
+            for k in range(nsup):
+                for s in relayed:
+                    chain_copy(listed[k].at[s], k, s, w).wait_send()
+
+        @pl.when((beyond(opposite, way) | (col == opposite)) & room(way) & far(opposite, way))
         def _():
             for k in range(nsup):
                 for s in relayed:
                     relay_copy(relay, s - relayed[0], k, s, w).wait_send()
 
-    @pl.when(col != opposite)
+    @pl.when(carries)
     def _():
         for k in range(nsup):
             for s in relayed:
@@ -316,9 +354,12 @@
             jax.ShapeDtypeStruct((nsup, BS, columns), narrow),
             jax.ShapeDtypeStruct(diag_inverse.shape, wide),
         ),
-        in_specs=[pl.BlockSpec(memory_space=pltpu.SMEM), vmem, vmem, vmem],
+        in_specs=[pl.BlockSpec(memory_space=pltpu.SMEM)] + [pl.BlockSpec(memory_space=pl.ANY)] * 3,
         out_specs=(vmem, vmem),
         scratch_shapes=[
+            pltpu.VMEM(ancestor_inverse.shape, narrow),
+            pltpu.VMEM((nsup, CAP, BS, columns), narrow),
+            pltpu.VMEM(diag_inverse.shape, wide),
             tuple(pltpu.VMEM((CAP, BS, columns), narrow) for _ in range(nsup)),
             pltpu.VMEM((nsup, RELAYED, BS, columns), narrow),
             pltpu.VMEM((nsup, columns, depth), narrow),
@@ -342,6 +383,7 @@
             dma((nsup, ncol - 1)),
             dma((nsup, ncol - 1)),
             dma((nsup,)),
+            dma((3,)),
         ],
         compiler_params=pltpu.CompilerParams(
             collective_id=0, has_side_effects=True, vmem_limit_bytes=48 * 1024 * 1024

time: 72.1 us -> 62.7 us (0.87)
  Pallas kernels: 65.6 us -> 56.2 us
    pallas_call x1, Pallas kernels: 65.6 us -> 56.2 us  [fused(): pl.pallas_call(functools.partial(kernel, ncol), out_shape=(jax.ShapeDtype...]
where the time goes in v2:
time: 62.7 us; the launch traced here: 62.5 us
  Pallas kernels  56.2 us (90%)
  local copies, waits for them, and re-layouts  5.59 us (9%)
  between operations  0.65 us (1%)
    pallas_call x1, Pallas kernels, fused(): pl.pallas_call(functools.partial(kernel, ncol), out_shape=(jax.ShapeDtype...  56.2 us
    unnamed x10, local copies, waits for them, and re-layouts  5.59 us

profile of v2, /device:TPU:0, one launch (start us, length us, event | category | flops | bytes accessed | tf_op | source)
XLA Modules:
  0.0 62.5 jit_solution(17058832527358398047)
XLA Ops:
  0.6 0.0 copy-start
  0.6 1.4 %copy-done = bf16[3,512,512]{2,1,0:T(8,128)(2,1)S(1)} copy-done((bf16[3,512,512]{2,1,0:T(8,128)(2,1)S(1)}, bf16[3,512,512]{2,1,0:T(8,128)(2,1)}, u32[]{:S(2)}) %copy-start) | copy-done | bytes 1572888
  2.0 0.0 copy-start.1
  2.0 1.2 %copy-done.1 = bf16[2,512,512]{2,1,0:T(8,128)(2,1)S(1)} copy-done((bf16[2,512,512]{2,1,0:T(8,128)(2,1)S(1)}, bf16[2,512,512]{2,1,0:T(8,128)(2,1)}, u32[]{:S(2)}) %copy-start.1) | copy-done | bytes 1048600
  3.3 0.0 copy-start.2
  3.3 0.9 %copy-done.2 = f32[3,16,512]{2,1,0:T(8,128)S(1)} copy-done((f32[3,16,512]{2,1,0:T(8,128)S(1)}, f32[3,16,512]{2,1,0:T(8,128)}, u32[]{:S(2)}) %copy-start.2) | copy-done | bytes 98328
  4.2 0.0 copy-start.3
  4.2 0.7 %copy-done.3 = s32[3,16]{1,0:T(4,128)S(1)} copy-done((s32[3,16]{1,0:T(4,128)S(1)}, s32[3,16]{1,0:T(4,128)}, u32[]{:S(2)}) %copy-start.3) | copy-done | bytes 216
  4.8 56.2 %shard_map.59 = (bf16[3,128,512]{2,1,0:T(8,128)(2,1)S(1)}, f32[3,16,512]{2,1,0:T(8,128)S(1)}) custom-call(s32[3,16]{1,0:T(4,128)S(1)} %copy-done.3, bf16[2,512,512]{2,1,0:T(8,128)(2,1)S(1)} %copy-done.1, bf16[3,4,128,512]{3,2,1,0:T(8,128)(2,1)S(1)} %bitcast.1, f32[3,16,512]{2,1,0:T(8,128)S(1)} %copy-done.2), custom_call_target="tpu_custom_call" | custom-call | tf_op jit(solution)/shard_map/pallas_call | solution.py:351
  61.1 0.7 %copy.8 = bf16[3,128,512]{2,1,0:T(8,128)(2,1)} copy(bf16[3,128,512]{2,1,0:T(8,128)(2,1)S(1)} %get-tuple-element.4) | data formatting | bytes 786432
  61.8 0.6 %copy.9 = f32[3,16,512]{2,1,0:T(8,128)} copy(f32[3,16,512]{2,1,0:T(8,128)S(1)} %get-tuple-element.5) | data formatting | bytes 196608
Async XLA Ops:
  0.6 1.4 %copy-start = (bf16[3,512,512]{2,1,0:T(8,128)(2,1)S(1)}, bf16[3,512,512]{2,1,0:T(8,128)(2,1)}, u32[]{:S(2)}) copy-start(bf16[3,512,512]{2,1,0:T(8,128)(2,1)} %param.5) | copy-start | bytes 4718596
  2.0 1.2 %copy-start.1 = (bf16[2,512,512]{2,1,0:T(8,128)(2,1)S(1)}, bf16[2,512,512]{2,1,0:T(8,128)(2,1)}, u32[]{:S(2)}) copy-start(bf16[2,512,512]{2,1,0:T(8,128)(2,1)} %inverse_hbm.1) | copy-start | bytes 3145732
  3.3 0.9 %copy-start.2 = (f32[3,16,512]{2,1,0:T(8,128)S(1)}, f32[3,16,512]{2,1,0:T(8,128)}, u32[]{:S(2)}) copy-start(f32[3,16,512]{2,1,0:T(8,128)} %diag_hbm.1) | copy-start | bytes 294916
  4.2 0.7 %copy-start.3 = (s32[3,16]{1,0:T(4,128)S(1)}, s32[3,16]{1,0:T(4,128)}, u32[]{:S(2)}) copy-start(s32[3,16]{1,0:T(4,128)} %lists.1) | copy-start | bytes 580
